TPU v7x, 128 devices: a whole 4x4x4 slice. The times are simulated.
128 devices in a mesh: row: 16 (over z, x_hi, core), col: 8 (over y, x_lo).
Axes of the slice: x: 4 (x_hi: 2, x_lo: 2; x = x_hi * 2 + x_lo), y: 4, z: 4, core: 2. Of those that a mesh axis runs over, the one named last changes fastest.
Arguments:
- tensor: float32 [1024, 8, 24576], P('row', 'col'), may hold values from -6 to 6
- occupancy: int32 [16, 8, 384], P('row', 'col'), may hold values 0 or 1
- coefficients: float32 [24576, 3072], P('row', 'col'), may hold values from -0.0390625 to 0.0390625
- coeff_occupancy: int32 [384, 48], P('row', 'col'), may hold values 0 or 1
Outputs:
- transformed: float32 [1024, 8, 3072], P('row', 'col')
All inputs are finite; a program needn't handle non-finite values. No bound on the sum of `occupancy` or of `coeff_occupancy` on one device may be relied on, other than what follows from the above.
Results may differ from a plain program's by a relative error of at most 0.00015.
Values sent between devices are 32-bit elements; how exact they have to be, the bound alone decides.
A program may use at most 128 MiB of HBM per device.

v0:
```python
import jax
import jax.numpy as jnp
from jax import lax
from jax.sharding import PartitionSpec as P

BLOCK = 64


def on_device(tensor, occupancy, coefficients, coeff_occupancy):
    mu_dev, p_dev, nu_all = tensor.shape
    shaped = tensor.reshape(mu_dev // BLOCK, BLOCK, p_dev, nu_all // BLOCK, BLOCK)
    weights = occupancy.astype(jnp.float32)[:, None, :, :, None]
    masked = (shaped * weights).reshape(mu_dev, p_dev, nu_all)
    regrouped = lax.all_to_all(masked, "row", split_axis=2, concat_axis=0, tiled=True)
    nu_dev, occ_dev = coefficients.shape
    coeff_shaped = coefficients.reshape(nu_dev // BLOCK, BLOCK, occ_dev // BLOCK, BLOCK)
    coeff_weights = coeff_occupancy.astype(jnp.float32)[:, None, :, None]
    masked_coeff = (coeff_shaped * coeff_weights).reshape(nu_dev, occ_dev)
    panels = lax.all_gather(masked_coeff, "col", axis=1, tiled=True)
    occ_all = panels.shape[1]
    count = mu_dev * lax.axis_size("row")
    flat = regrouped.reshape(count * p_dev, nu_dev)
    product = jnp.dot(
        flat, panels, preferred_element_type=jnp.float32, precision=lax.Precision.HIGHEST
    )
    return lax.psum_scatter(
        product.reshape(count, p_dev, occ_all), "row", scatter_dimension=0, tiled=True
    )


def solution(mesh):
    in_specs = (P("row", "col", None), P("row", "col", None), P("row", "col"), P("row", "col"))
    out_specs = P("row", "col", None)
    return jax.shard_map(
        on_device, mesh=mesh, in_specs=in_specs, out_specs=out_specs, check_vma=False
    )
```

profile of v0, /device:TPU:0, one launch (start us, length us, event | category | flops | bytes accessed | tf_op | source)
XLA Modules:
  0.0 657.4 jit_solution(4457008324632523983)
XLA Ops:
  6.5 0.7 convert_element_type.7
  7.2 2.5 mul.33
  9.7 3.6 mul.34
  13.4 3.1 copy.27
  16.5 3.4 mul.35
  20.0 0.0 all-gather.2.cloned.1.call-update
  20.0 0.0 reduce-scatter.2.cloned.1.call-start
  20.1 0.1 mul.29
  20.2 0.1 mul.30
  20.3 9.1 %copy_multiply_fusion = f32[64,1,24576]{2,0,1:T(8,128)} fusion(f32[64,1,24576]{2,1,0:T(1,128)} %param.4, f32[24576]{0:T(1024)S(1)} %mul.30), kind=kLoop, calls=%fused_computation.1 | loop fusion | flops 1572864 | bytes 12681216 | tf_op jit(solution)/shard_map/mul | solution.py:13
  29.4 25.2 %copy.24 = f32[64,1,24576]{0,1,2:T(1,128)} copy(f32[64,1,24576]{2,0,1:T(8,128)} %copy_multiply_fusion) | data formatting | bytes 12582912 | tf_op jit(solution)/shard_map/mul | solution.py:13
  54.5 0.5 broadcast.8
  55.1 110.6 %reduce.2 = f32[24576,64]{1,0:T(8,128)} reduce(f32[24576,1,64]{2,1,0:T(1,128)} %bitcast.14, f32[]{:T(128)} %broadcast.8), dimensions={1}, to_apply=%bitcast.9.reduce_sub_computation | reduce | bytes 12582916
  165.7 15.9 %reshape.23 = f32[16,1,98304]{2,1,0:T(1,128)} reshape(f32[24576,64]{1,0:T(8,128)} %reduce.2) | data formatting | bytes 12582912
  181.5 150.0 %all_to_all.15 = f32[16,1,98304]{2,1,0:T(1,128)} all-to-all(f32[16,1,98304]{2,1,0:T(1,128)} %reshape.23), channel_id=1, replica_groups=mesh['row'=16,'col'=8] {'row'}, dimensions={0} | all-to-all | bytes 12582912 | tf_op jit(solution)/shard_map/all_to_all | solution.py:14
  331.5 19.5 %reduce.3 = f32[16,98304]{1,0:T(8,128)} reduce(f32[16,1,98304]{2,1,0:T(1,128)} %all_to_all.15, f32[]{:T(128)} %broadcast.8), dimensions={1}, to_apply=%all_to_all.11.reduce_sub_computation | reduce | bytes 12582916 | tf_op jit(solution)/shard_map/all_to_all | solution.py:14
  351.0 22.6 %reshape.24 = f32[24576,1,64]{2,1,0:T(1,128)} reshape(f32[16,98304]{1,0:T(8,128)} %reduce.3) | data formatting | bytes 12582912
  373.6 10.5 %copy.29 = f32[64,1,16,1536]{3,2,0,1:T(8,128)} copy(f32[64,1,16,1536]{0,3,2,1:T(8,128)} %bitcast.13) | data formatting | bytes 12582912 | tf_op jit(solution)/shard_map/all_to_all | solution.py:14
  384.1 9.1 %copy.26 = f32[16,64,1,1536]{3,1,0,2:T(8,128)} copy(f32[16,64,1,1536]{3,0,1,2:T(8,128)} %bitcast.15) | data formatting | bytes 12582912 | tf_op jit(solution)/shard_map/all_to_all | solution.py:14
  393.2 61.7 %all-gather.2.cloned.1.call-done = f32[1536,3072]{0,1:T(8,128)} async-done(((f32[1536,384]{0,1:T(8,128)}), f32[1536,3072]{0,1:T(8,128)}) %all-gather.2.cloned.1.call-update) | async-done | bytes 18874384 | tf_op jit(solution)/shard_map/all_gather | solution.py:19
  454.9 69.1 %convolution_bitcast_fusion = f32[1024,1,3072]{2,0,1:T(8,128)} fusion(f32[1024,1536]{1,0:T(8,128)} %bitcast.16, f32[1536,3072]{0,1:T(8,128)} %all-gather.2.cloned.1.call-done), kind=kOutput, calls=%fused_computation | convolution fusion | flops 57982058496 | bytes 37748736 | tf_op jit(solution)/shard_map/dot_general | solution.py:23
  524.0 0.0 reduce-scatter.2.cloned.1.call-update
  524.1 123.7 %reduce-scatter.2.cloned.1.call-done = f32[64,1,3072]{2,0,1:T(8,128)} async-done(((f32[1024,1,3072]{2,0,1:T(8,128)}), f32[64,1,3072]{2,0,1:T(8,128)}) %reduce-scatter.2.cloned.1.call-update) | async-done | bytes 786448 | tf_op jit(solution)/shard_map/reduce_scatter | solution.py:26
  647.7 2.8 copy.28
  (4 shorter events, 0.0 us)
Async XLA Ops:
  6.5 448.4 %all-gather.2.cloned.1.call-start = ((), (), s32[]{:S(2)}) async-start(), calls=%async_computation.2 | async-start | bytes 21233664 | tf_op jit(solution)/shard_map/all_gather | solution.py:19
  13.4 6.7 %copy-start = (s32[1,1,384]{2,1,0:T(1,128)S(1)}, s32[1,1,384]{2,1,0:T(1,128)}, u32[]{:S(2)}) copy-start(s32[1,1,384]{2,1,0:T(1,128)} %param.5) | copy-start | bytes 4612
  20.0 627.7 %reduce-scatter.2.cloned.1.call-start = ((), (), s32[]{:S(2)}) async-start(), calls=%async_computation.3 | async-start | bytes 13369344 | tf_op jit(solution)/shard_map/reduce_scatter | solution.py:26
Sparse Core Ops, SparseCore 0:
  20.1 434.7 all-gather.1
  524.2 123.5 reduce-scatter.1
where the time goes:
time: 659 us; the launch traced here: 657 us
  waiting for transfers between devices  185 us (28%)
  blocking collectives  150 us (23%)
  other arithmetic  143 us (22%)
  local copies, waits for them, and re-layouts  96.1 us (15%)
  matrix products  69.1 us (10%)
  between operations  13.4 us (2%)
    all_to_all x1, blocking collectives, on_device(): lax.all_to_all(masked, 'row', split_axis=2, concat_axis=0, tiled=True)  150 us
    reduce_scatter x1, waiting for transfers between devices, on_device(): lax.psum_scatter(product.reshape(count, p_dev, occ_all), 'row', scatter_d...  124 us
    unnamed x1, other arithmetic  111 us
    dot_general x1, matrix products, on_device(): jnp.dot(flat, panels, preferred_element_type=jnp.float32, precision=lax.P...  69.1 us
    all_gather x1, waiting for transfers between devices, on_device(): panels = lax.all_gather(masked_coeff, 'col', axis=1, tiled=True)  61.7 us
    unnamed x6, local copies, waits for them, and re-layouts  42.1 us
    mul x3, local copies, waits for them, and re-layouts, on_device(): masked = (shaped * weights).reshape(mu_dev, p_dev, nu_all)  25.4 us
    all_to_all x2, local copies, waits for them, and re-layouts, on_device(): lax.all_to_all(masked, 'row', split_axis=2, concat_axis=0, tiled=True)  19.6 us
  transfers between devices with their start and end apart: 2, of which 2 were waited for; matrix products, arithmetic and copies ran while one was open for 34% of the time, Pallas kernels for 0%

commit v1 on v0

v1 whole, which is shorter than its diff:
```python
import functools

import jax
import jax.numpy as jnp
from jax import lax
from jax.experimental import pallas as pl
from jax.experimental.pallas import tpu as pltpu
from jax.sharding import PartitionSpec as P

BLOCK = 64
MESH = pl.DeviceIdType.MESH
PIECES = 4
OFFSETS = [(ez, eh, ec) for eh in range(2) for ec in range(2) for ez in range(4)]
PANELS = [(0, 0), (0, 1), (3, 0), (1, 0), (3, 1), (1, 1), (2, 0), (2, 1)]
TASKS = [(0, 0), (1, 0), (2, 0), (3, 0), (0, 1), (1, 1), (2, 1), (3, 1),
         (4, 0), (4, 1), (5, 0), (5, 1), (6, 0), (6, 1), (7, 0), (7, 1)]


def place(offset):
    ez, eh, ec = offset
    return eh * 8 + ec * 4 + ez


def opposite(offset):
    ez, eh, ec = offset
    return ((4 - ez) % 4, eh, ec)


def kernel(a_hbm, amask, b_hbm, bmask, out_ref, astage, arecv, ahi, alo, bbuf, bhi, blo, cpart, crecv, zrecv, keep, xrecv,
           al_sem, as_sem, ar_sem, bl_sem, bs_sem, br_sem, cs_sem, cr_sem, zs_sem, zr_sem, xs_sem, xr_sem):
    depth, width = bbuf.shape[1:]
    chunk = depth // PIECES
    r, c = lax.axis_index("row"), lax.axis_index("col")
    z, xh, core = r // 4, (r // 2) % 2, r % 2
    y, xl = c // 2, c % 2

    def row_of(offset):
        ez, eh, ec = offset
        return ((z + ez) % 4) * 4 + ((xh + eh) % 2) * 2 + (core + ec) % 2

    def col_of(ey, el):
        return ((y + ey) % 4) * 2 + (xl + el) % 2

    def remote(src, dst, send, recv, device):
        return pltpu.make_async_remote_copy(src_ref=src, dst_ref=dst, send_sem=send, recv_sem=recv,
                                            device_id=device, device_id_type=MESH)

    up, down, pair = (r, col_of(1, 0)), (r, col_of(3, 0)), (r, col_of(0, 1))

    def b_load(k):
        rows = pl.ds(k * chunk, chunk)
        return pltpu.make_async_copy(b_hbm.at[rows], bbuf.at[0, rows], bl_sem.at[k])

    def a_load(offset):
        i = place(offset)
        cols = pl.ds(pl.multiple_of(row_of(offset) * depth, 128), depth)
        return pltpu.make_async_copy(a_hbm.at[:, cols], astage.at[i], al_sem.at[i])

    order = (0, 2, 1, 3)
    for k in order:
        b_load(k).start()
    send_order = sorted(OFFSETS, key=lambda o: (o[1] == 0, o[0] == 0, o[2]))
    for offset in send_order:
        a_load(offset).start()

    barrier = pltpu.get_barrier_semaphore()
    partners = [(row_of(o), c) for o in OFFSETS[1:]] + [up, down, pair]
    for device in partners:
        pl.semaphore_signal(barrier, inc=1, device_id=device, device_id_type=MESH)
    pl.semaphore_wait(barrier, len(partners))

    def b_copy(src, dst, k, device, sends):
        rows = pl.ds(k * chunk, chunk)
        return remote(bbuf.at[src, rows], bbuf.at[dst, rows], bs_sem.at[sends, k], br_sem.at[dst, k], device)

    own_up = [b_copy(0, 2, k, up, 0) for k in range(PIECES)]
    own_down = [b_copy(0, 3, k, down, 1) for k in range(PIECES)]
    own_pair = [b_copy(0, 1, k, pair, 2) for k in range(PIECES)]
    pair_up = [b_copy(1, 4, k, up, 3) for k in range(PIECES)]
    pair_down = [b_copy(1, 5, k, down, 4) for k in range(PIECES)]
    half = PIECES // 2
    on_own = [b_copy(2, 6, k, up, 5) if k < half else b_copy(3, 6, k, down, 5) for k in range(PIECES)]
    on_pair = [b_copy(4, 7, k, up, 6) if k < half else b_copy(5, 7, k, down, 6) for k in range(PIECES)]

    per = chunk // BLOCK
    for k in order:
        b_load(k).wait()
        for j in range(per):
            rows = pl.ds(k * chunk + j * BLOCK, BLOCK)
            bbuf[0, rows, :] = bbuf[0, rows, :] * bmask[k * per + j:k * per + j + 1, :]
        own_pair[k].start()
        own_up[k].start()
        own_down[k].start()

    def a_copy(offset):
        i, j = place(offset), place(opposite(offset))
        return remote(astage.at[i], arecv.at[j], as_sem.at[i], ar_sem.at[j], (row_of(offset), c))

    def split(values, i):
        high = values.astype(jnp.bfloat16)
        rows = pl.ds(i * BLOCK, BLOCK)
        ahi[rows, :] = high
        alo[rows, :] = (values - high.astype(jnp.float32)).astype(jnp.bfloat16)

    for offset in send_order:
        i = place(offset)
        a_load(offset).wait()
        masked = astage[i] * amask[pl.ds(row_of(offset), 1), :]
        if i == 0:
            split(masked, 0)
        else:
            astage[i] = masked
            a_copy(offset).start()

    def take(h):
        for offset in OFFSETS:
            i = place(offset)
            if i > 0 and offset[1] == h:
                a_copy(opposite(offset)).wait_recv()
                split(arecv[i], i)

    def multiply(t):
        n, h = TASKS[t]
        slot = t % 2
        if t >= 2:
            c_copy(t - 2).wait_send()

        def convert(j, _):
            rows = pl.ds(pl.multiple_of(j * BLOCK, BLOCK), BLOCK)
            values = bbuf[n, rows, :]
            high = values.astype(jnp.bfloat16)
            bhi[rows, :] = high
            blo[rows, :] = (values - high.astype(jnp.float32)).astype(jnp.bfloat16)
            return _

        lax.fori_loop(0, depth // BLOCK, convert, 0)

        def tile(m, _):
            rows = pl.ds(pl.multiple_of(h * 512 + m * 256, 256), 256)
            high, low = ahi[rows, :], alo[rows, :]
            total = jnp.dot(low, bhi[...], preferred_element_type=jnp.float32)
            total += jnp.dot(high, blo[...], preferred_element_type=jnp.float32)
            total += jnp.dot(high, bhi[...], preferred_element_type=jnp.float32)
            cpart[slot, pl.ds(m * 4, 4)] = total.reshape(4, BLOCK, width)
            return _

        lax.fori_loop(0, 2, tile, 0)
        c_copy(t).start()

    other = (row_of((0, 0, 1)), c)

    def c_copy(t):
        return remote(cpart.at[t % 2, pl.ds(4, 4)], crecv.at[t], cs_sem.at[t], cr_sem.at[t], other)

    def z_copy(t, ez):
        return remote(crecv.at[t, ez], zrecv.at[t, ez - 1], zs_sem.at[t, ez - 1], zr_sem.at[t, ez - 1],
                      (row_of((ez, 0, 0)), c))

    def x_copy(t):
        n = TASKS[t][0]
        return remote(keep.at[1, n], xrecv.at[n], xs_sem.at[n], xr_sem.at[n], (row_of((0, 1, 0)), c))

    def over_cores(t):
        c_copy(t).wait_recv()
        crecv[t] = crecv[t] + cpart[t % 2, pl.ds(0, 4)]
        for ez in (2, 1, 3):
            z_copy(t, ez).start()

    def over_z(t):
        n, h = TASKS[t]
        for ez in (1, 2, 3):
            z_copy(t, ez).wait_recv()
        keep[h, n] = (crecv[t, 0] + zrecv[t, 0]) + (zrecv[t, 1] + zrecv[t, 2])
        if h == 1:
            x_copy(t).start()

    def finish(t):
        n, h = TASKS[t]
        if h == 0:
            return
        x_copy(t).wait_recv()
        cols = pl.ds(pl.multiple_of(col_of(*PANELS[n]) * width, 128), width)
        out_ref[:, cols] = keep[0, n] + xrecv[n]

    def forward_own():
        for k in (0, 2, 1, 3):
            (own_up if k < half else own_down)[k].wait_recv()
            on_own[k].start()

    def forward_pair():
        for k in order:
            own_pair[k].wait_recv()
            pair_up[k].start()
            pair_down[k].start()

    def pass_on_pair():
        for k in (0, 2, 1, 3):
            (pair_up if k < half else pair_down)[k].wait_recv()
            on_pair[k].start()

    def rest(copies, ks):
        for k in ks:
            copies[k].wait_recv()

    before = {
        0: lambda: (forward_own(), take(0)),
        1: forward_pair,
        2: lambda: rest(own_up, range(half, PIECES)),
        3: lambda: rest(own_down, range(half)),
        4: lambda: take(1),
        8: lambda: (pass_on_pair(), rest(pair_up, range(half, PIECES))),
        10: lambda: rest(pair_down, range(half)),
        12: lambda: rest(on_own, range(PIECES)),
        14: lambda: rest(on_pair, range(PIECES)),
    }
    count = len(TASKS)
    for t in range(count + 4):
        if t in before:
            before[t]()
        if t < count:
            multiply(t)
        if 0 <= t - 1 < count:
            over_cores(t - 1)
        if 0 <= t - 2 < count:
            over_z(t - 2)
        if 0 <= t - 4 < count:
            finish(t - 4)

    for copies in (own_up, own_down, own_pair, pair_up, pair_down, on_own, on_pair):
        for copy in copies:
            copy.wait_send()
    for offset in OFFSETS[1:]:
        a_copy(offset).wait_send()
    for t in (count - 2, count - 1):
        c_copy(t).wait_send()
    for t in range(count):
        for ez in (1, 2, 3):
            z_copy(t, ez).wait_send()
        if TASKS[t][1] == 1:
            x_copy(t).wait_send()


def on_device(tensor, occupancy, coefficients, coeff_occupancy):
    mu_dev, p_dev, nu_all = tensor.shape
    depth, width = coefficients.shape
    count = nu_all // depth
    amask = jnp.repeat(occupancy.astype(jnp.float32).reshape(count, depth // BLOCK), BLOCK, axis=1)
    bmask = jnp.repeat(coeff_occupancy.astype(jnp.float32), BLOCK, axis=1)
    panels, tasks = len(PANELS), len(TASKS)
    f32, bf16, dma = jnp.float32, jnp.bfloat16, pltpu.SemaphoreType.DMA
    vmem, hbm = pl.BlockSpec(memory_space=pltpu.VMEM), pl.BlockSpec(memory_space=pl.ANY)
    result = pl.pallas_call(
        kernel,
        out_shape=jax.ShapeDtypeStruct((mu_dev, panels * width), f32),
        in_specs=[hbm, vmem, hbm, vmem],
        out_specs=vmem,
        scratch_shapes=[
            pltpu.VMEM((count, mu_dev, depth), f32),
            pltpu.VMEM((count, mu_dev, depth), f32),
            pltpu.VMEM((count * mu_dev, depth), bf16),
            pltpu.VMEM((count * mu_dev, depth), bf16),
            pltpu.VMEM((panels, depth, width), f32),
            pltpu.VMEM((depth, width), bf16),
            pltpu.VMEM((depth, width), bf16),
            pltpu.VMEM((2, 8, mu_dev, width), f32),
            pltpu.VMEM((tasks, 4, mu_dev, width), f32),
            pltpu.VMEM((tasks, 3, mu_dev, width), f32),
            pltpu.VMEM((2, panels, mu_dev, width), f32),
            pltpu.VMEM((panels, mu_dev, width), f32),
            dma((count,)), dma((count,)), dma((count,)),
            dma((PIECES,)), dma((7, PIECES)), dma((panels, PIECES)),
            dma((tasks,)), dma((tasks,)), dma((tasks, 3)), dma((tasks, 3)),
            dma((panels,)), dma((panels,)),
        ],
        compiler_params=pltpu.CompilerParams(
            collective_id=0, has_side_effects=True, vmem_limit_bytes=62 * 1024 * 1024),
        cost_estimate=pl.CostEstimate(
            flops=6 * count * mu_dev * depth * panels * width, bytes_accessed=16 * 1024 * 1024, transcendentals=0),
        name="transform",
    )(tensor.reshape(mu_dev * p_dev, nu_all), amask, coefficients, bmask)
    return result.reshape(mu_dev, p_dev, panels * width)


def solution(mesh):
    in_specs = (P("row", "col", None), P("row", "col", None), P("row", "col"), P("row", "col"))
    out_specs = P("row", "col", None)
    return jax.shard_map(
        on_device, mesh=mesh, in_specs=in_specs, out_specs=out_specs, check_vma=False
    )
```

time: 659 us -> 218 us (0.33)
  Pallas kernels: 0 us -> 202 us
  waiting for transfers between devices: 185 us -> 0 us
  blocking collectives: 150 us -> 0 us
  other arithmetic: 143 us -> 1.39 us
  local copies, waits for them, and re-layouts: 96.1 us -> 13.6 us
  matrix products: 69.1 us -> 0 us
  between operations: 13.4 us -> 0.04 us
    pallas_call x0 -> x1, Pallas kernels: none -> 202 us  [on_device(): pl.pallas_call(kernel, out_shape=jax.ShapeDtypeStruct((mu_dev, panels * w...]
    all_to_all x1 -> x0, blocking collectives: 150 us -> none  [on_device(): lax.all_to_all(masked, 'row', split_axis=2, concat_axis=0, tiled=True)]
    reduce_scatter x1 -> x0, waiting for transfers between devices: 124 us -> none  [on_device(): lax.psum_scatter(product.reshape(count, p_dev, occ_all), 'row', scatter_d...]
    unnamed x1 -> x0, other arithmetic: 111 us -> none
    dot_general x1 -> x0, matrix products: 69.1 us -> none  [on_device(): jnp.dot(flat, panels, preferred_element_type=jnp.float32, precision=lax.P...]
    all_gather x1 -> x0, waiting for transfers between devices: 61.7 us -> none  [on_device(): panels = lax.all_gather(masked_coeff, 'col', axis=1, tiled=True)]
    unnamed x6 -> x1, local copies, waits for them, and re-layouts: 42.1 us -> 9 us
    mul x5 -> x0, local copies, waits for them, and re-layouts: 31.5 us -> none  [the longest x3 25.4 us: on_device(): masked = (shaped * weights).reshape(mu_dev, p_dev, nu_all)]
  transfers between devices with their start and end apart: 2 -> 0, of which waited for: 2 -> 0; matrix products, arithmetic and copies ran while one was open for 34% -> 0% of each run, Pallas kernels for 0% -> 0%
where the time goes in v1:
time: 218 us; the launch traced here: 217 us
  Pallas kernels  202 us (93%)
  local copies, waits for them, and re-layouts  13.6 us (6%)
    pallas_call x1, Pallas kernels, on_device(): pl.pallas_call(kernel, out_shape=jax.ShapeDtypeStruct((mu_dev, panels * w...  202 us
    unnamed x1, local copies, waits for them, and re-layouts  9 us

profile of v1, /device:TPU:0, one launch (start us, length us, event | category | flops | bytes accessed | tf_op | source)
XLA Modules:
  0.0 217.4 jit_solution(9762195888358906855)
XLA Ops:
  0.0 0.7 convert_reduce_fusion
  0.7 0.7 convert_element_type.7
  1.4 0.1 reshape.16
  1.5 0.1 copy.7
  1.6 0.1 broadcast_in_dim.7
  1.6 0.7 reshape.18.bmask
  2.3 0.1 broadcast_in_dim.6
  2.5 0.7 reshape.17.amask
  3.2 9.0 %copy.11 = f32[64,1,24576]{2,0,1:T(8,128)} copy(f32[64,1,24576]{2,1,0:T(1,128)} %param.4) | data formatting | bytes 12582912
  12.2 202.4 %transform.1 = f32[64,3072]{1,0:T(8,128)} custom-call(f32[64,24576]{1,0:T(8,128)} %bitcast.4, f32[16,1536]{1,0:T(8,128)} %reshape.17.amask, f32[1536,384]{1,0:T(8,128)} %b_hbm.1, f32[24,384]{1,0:T(8,128)} %reshape.18.bmask), custom_call_target="tpu_custom_call" | custom-call | flops 28991029248 | bytes 16777216 | tf_op jit(solution)/shard_map/transform/pallas_call | solution.py:252
  214.6 2.8 %copy.8 = f32[64,1,3072]{2,1,0:T(1,128)} copy(f32[64,1,3072]{2,0,1:T(8,128)} %bitcast.5) | data formatting | bytes 1572864 | tf_op jit(solution)/shard_map/reshape | solution.py:281

commit v2 on v1

--- a/solution.py
+++ b/solution.py
@@ -10,10 +10,15 @@
 BLOCK = 64
 MESH = pl.DeviceIdType.MESH
 PIECES = 4
+SLOTS = 3
+CORE_LAG = 1
+PASS_LAG = 3
+Z_LAG = 5
+X_LAG = 7
 OFFSETS = [(ez, eh, ec) for eh in range(2) for ec in range(2) for ez in range(4)]
 PANELS = [(0, 0), (0, 1), (3, 0), (1, 0), (3, 1), (1, 1), (2, 0), (2, 1)]
-TASKS = [(0, 0), (1, 0), (2, 0), (3, 0), (0, 1), (1, 1), (2, 1), (3, 1),
-         (4, 0), (4, 1), (5, 0), (5, 1), (6, 0), (6, 1), (7, 0), (7, 1)]
+TASKS = [(0, 0), (2, 0), (3, 0), (1, 0), (6, 0), (0, 1), (2, 1), (3, 1), (1, 1), (6, 1),
+         (4, 0), (4, 1), (5, 0), (5, 1), (7, 1), (7, 0)]
 
 
 def place(offset):
@@ -26,7 +31,7 @@
     return ((4 - ez) % 4, eh, ec)
 
 
-def kernel(a_hbm, amask, b_hbm, bmask, out_ref, astage, arecv, ahi, alo, bbuf, bhi, blo, cpart, crecv, zrecv, keep, xrecv,
+def kernel(a_hbm, aocc, b_hbm, bocc, out_ref, araw, astage, arecv, ahi, alo, bbuf, bhi, blo, cpart, crecv, zrecv, keep, xrecv,
            al_sem, as_sem, ar_sem, bl_sem, bs_sem, br_sem, cs_sem, cr_sem, zs_sem, zr_sem, xs_sem, xr_sem):
     depth, width = bbuf.shape[1:]
     chunk = depth // PIECES
@@ -51,17 +56,19 @@
         rows = pl.ds(k * chunk, chunk)
         return pltpu.make_async_copy(b_hbm.at[rows], bbuf.at[0, rows], bl_sem.at[k])
 
-    def a_load(offset):
-        i = place(offset)
-        cols = pl.ds(pl.multiple_of(row_of(offset) * depth, 128), depth)
-        return pltpu.make_async_copy(a_hbm.at[:, cols], astage.at[i], al_sem.at[i])
+    strips = depth // 128
+    chips = [(2, 0), (1, 0), (3, 0), (0, 0), (2, 1), (1, 1), (3, 1), (0, 1)]
+
+    def a_load(j):
+        ez, eh = chips[j]
+        rows = pl.ds(pl.multiple_of(row_of((ez, eh, 0)) // 2 * 2 * strips, 8), 2 * strips)
+        return pltpu.make_async_copy(a_hbm.at[:, rows], araw.at[j % SLOTS], al_sem.at[j])
 
     order = (0, 2, 1, 3)
     for k in order:
         b_load(k).start()
-    send_order = sorted(OFFSETS, key=lambda o: (o[1] == 0, o[0] == 0, o[2]))
-    for offset in send_order:
-        a_load(offset).start()
+    for j in range(SLOTS):
+        a_load(j).start()
 
     barrier = pltpu.get_barrier_semaphore()
     partners = [(row_of(o), c) for o in OFFSETS[1:]] + [up, down, pair]
@@ -82,12 +89,23 @@
     on_own = [b_copy(2, 6, k, up, 5) if k < half else b_copy(3, 6, k, down, 5) for k in range(PIECES)]
     on_pair = [b_copy(4, 7, k, up, 6) if k < half else b_copy(5, 7, k, down, 6) for k in range(PIECES)]
 
+    left = lax.broadcasted_iota(jnp.int32, (1, 128), 1) < BLOCK
+
+    def weight(first, second):
+        return jnp.where(left, first, second).astype(jnp.float32)
+
     per = chunk // BLOCK
     for k in order:
         b_load(k).wait()
-        for j in range(per):
-            rows = pl.ds(k * chunk + j * BLOCK, BLOCK)
-            bbuf[0, rows, :] = bbuf[0, rows, :] * bmask[k * per + j:k * per + j + 1, :]
+
+        def mask_rows(j, _):
+            rows = pl.ds(pl.multiple_of(j * BLOCK, BLOCK), BLOCK)
+            for l in range(width // 128):
+                cols = pl.ds(l * 128, 128)
+                bbuf[0, rows, cols] = bbuf[0, rows, cols] * weight(bocc[2 * l, j], bocc[2 * l + 1, j])
+            return _
+
+        lax.fori_loop(k * per, (k + 1) * per, mask_rows, 0)
         own_pair[k].start()
         own_up[k].start()
         own_down[k].start()
@@ -102,15 +120,34 @@
         ahi[rows, :] = high
         alo[rows, :] = (values - high.astype(jnp.float32)).astype(jnp.bfloat16)
 
-    for offset in send_order:
-        i = place(offset)
-        a_load(offset).wait()
-        masked = astage[i] * amask[pl.ds(row_of(offset), 1), :]
-        if i == 0:
-            split(masked, 0)
-        else:
-            astage[i] = masked
-            a_copy(offset).start()
+    for j, (ez, eh) in enumerate(chips):
+        a_load(j).wait()
+        raw = araw.at[j % SLOTS].reshape(BLOCK * 2 * strips, 128)
+        for ec in (1, 0):
+            offset = (ez, eh, ec)
+            i, row = place(offset), row_of(offset)
+            first = row * (depth // BLOCK)
+            weights = [weight(aocc[0, first + 2 * l], aocc[0, first + 2 * l + 1]) for l in range(strips)]
+
+            def strip(g, _):
+                rows = pl.ds(pl.multiple_of(g * 8, 8), 8)
+                start = g * (16 * strips) + (row % 2) * strips
+                for l in range(strips):
+                    astage[i, rows, pl.ds(l * 128, 128)] = raw[pl.ds(start + l, 8, stride=2 * strips), :] * weights[l]
+                return _
+
+            lax.fori_loop(0, BLOCK // 8, strip, 0)
+            if i == 0:
+                split(astage[0], 0)
+            elif eh == 0:
+                a_copy(offset).start()
+        if j + SLOTS < len(chips):
+            a_load(j + SLOTS).start()
+
+    for offset in OFFSETS[1:8]:
+        a_copy(offset).wait_send()
+    for offset in sorted(OFFSETS[8:], key=lambda o: -o[0] % 4 == 2):
+        a_copy(offset).start()
 
     def take(h):
         for offset in OFFSETS:
@@ -152,9 +189,17 @@
     def c_copy(t):
         return remote(cpart.at[t % 2, pl.ds(4, 4)], crecv.at[t], cs_sem.at[t], cr_sem.at[t], other)
 
-    def z_copy(t, ez):
-        return remote(crecv.at[t, ez], zrecv.at[t, ez - 1], zs_sem.at[t, ez - 1], zr_sem.at[t, ez - 1],
-                      (row_of((ez, 0, 0)), c))
+    ahead, behind = (row_of((1, 0, 0)), c), (row_of((3, 0, 0)), c)
+
+    def z_copy(t, k):
+        low, high = pl.ds(0, BLOCK // 2), pl.ds(BLOCK // 2, BLOCK // 2)
+        src, dst, device = [
+            (crecv.at[t, 2, low], zrecv.at[t, 0, low], ahead),
+            (crecv.at[t, 2, high], zrecv.at[t, 0, high], behind),
+            (crecv.at[t, 1], zrecv.at[t, 1], ahead),
+            (crecv.at[t, 3], zrecv.at[t, 2], behind),
+        ][k]
+        return remote(src, dst, zs_sem.at[t, k], zr_sem.at[t, k], device)
 
     def x_copy(t):
         n = TASKS[t][0]
@@ -162,25 +207,64 @@
 
     def over_cores(t):
         c_copy(t).wait_recv()
-        crecv[t] = crecv[t] + cpart[t % 2, pl.ds(0, 4)]
-        for ez in (2, 1, 3):
-            z_copy(t, ez).start()
+        crecv[t, 2] = crecv[t, 2] + cpart[t % 2, 2]
+        z_copy(t, 0).start()
+        z_copy(t, 1).start()
+        for ez in (1, 3, 0):
+            crecv[t, ez] = crecv[t, ez] + cpart[t % 2, ez]
+
+    def pass_on(t):
+        for k, ez, rows in ((0, 1, pl.ds(0, BLOCK // 2)), (1, 3, pl.ds(BLOCK // 2, BLOCK // 2))):
+            z_copy(t, k).wait_recv()
+            crecv[t, ez, rows, :] = crecv[t, ez, rows, :] + zrecv[t, 0, rows, :]
+            z_copy(t, k + 2).start()
 
     def over_z(t):
         n, h = TASKS[t]
-        for ez in (1, 2, 3):
-            z_copy(t, ez).wait_recv()
-        keep[h, n] = (crecv[t, 0] + zrecv[t, 0]) + (zrecv[t, 1] + zrecv[t, 2])
+        z_copy(t, 2).wait_recv()
+        z_copy(t, 3).wait_recv()
+        keep[h, n] = crecv[t, 0] + (zrecv[t, 1] + zrecv[t, 2])
         if h == 1:
             x_copy(t).start()
 
     def finish(t):
-        n, h = TASKS[t]
-        if h == 0:
+        n, _ = TASKS[t]
+        if n not in [task[0] for task in TASKS[:t]]:
             return
         x_copy(t).wait_recv()
         cols = pl.ds(pl.multiple_of(col_of(*PANELS[n]) * width, 128), width)
         out_ref[:, cols] = keep[0, n] + xrecv[n]
+
+    def multiply_last():
+        t0 = len(TASKS) - 2
+        n = TASKS[t0][0]
+        for t in (t0 - 2, t0 - 1):
+            c_copy(t).wait_send()
+        for step, k in enumerate(order):
+            on_pair[k].wait_recv()
+            ks = pl.ds(k * chunk, chunk)
+            values = bbuf[n, ks, :]
+            high = values.astype(jnp.bfloat16)
+            bhi[ks, :] = high
+            blo[ks, :] = (values - high.astype(jnp.float32)).astype(jnp.bfloat16)
+            for t in (t0, t0 + 1):
+                h = TASKS[t][1]
+
+                def tile(m, _):
+                    rows = pl.ds(pl.multiple_of(h * 512 + m * 256, 256), 256)
+                    high, low = ahi[rows, ks], alo[rows, ks]
+                    total = jnp.dot(low, bhi[ks, :], preferred_element_type=jnp.float32)
+                    total += jnp.dot(high, blo[ks, :], preferred_element_type=jnp.float32)
+                    total += jnp.dot(high, bhi[ks, :], preferred_element_type=jnp.float32)
+                    total = total.reshape(4, BLOCK, width)
+                    if step > 0:
+                        total += cpart[t % 2, pl.ds(m * 4, 4)]
+                    cpart[t % 2, pl.ds(m * 4, 4)] = total
+                    return _
+
+                lax.fori_loop(0, 2, tile, 0)
+                if step == PIECES - 1:
+                    c_copy(t).start()
 
     def forward_own():
         for k in (0, 2, 1, 3):
@@ -193,8 +277,8 @@
             pair_up[k].start()
             pair_down[k].start()
 
-    def pass_on_pair():
-        for k in (0, 2, 1, 3):
+    def pass_on_pair(ks):
+        for k in ks:
             (pair_up if k < half else pair_down)[k].wait_recv()
             on_pair[k].start()
 
@@ -202,40 +286,49 @@
         for k in ks:
             copies[k].wait_recv()
 
+    count = len(TASKS)
+    done = set()
+
+    def advance(stage, t):
+        if (stage, t) not in done:
+            done.add((stage, t))
+            stage(t)
+
+    def flush(end):
+        for stage in (over_cores, pass_on, over_z, finish):
+            for t in range(end):
+                advance(stage, t)
+
     before = {
-        0: lambda: (forward_own(), take(0)),
-        1: forward_pair,
-        2: lambda: rest(own_up, range(half, PIECES)),
-        3: lambda: rest(own_down, range(half)),
-        4: lambda: take(1),
-        8: lambda: (pass_on_pair(), rest(pair_up, range(half, PIECES))),
-        10: lambda: rest(pair_down, range(half)),
-        12: lambda: rest(on_own, range(PIECES)),
-        14: lambda: rest(on_pair, range(PIECES)),
+        0: lambda: take(0),
+        1: lambda: (forward_own(), forward_pair(), rest(own_up, range(half, PIECES)), rest(own_down, range(half))),
+        4: lambda: (flush(4), rest(on_own, range(PIECES))),
+        5: lambda: (flush(5), take(1)),
+        8: lambda: pass_on_pair((0, 2, 1, 3)),
+        10: lambda: rest(pair_up, range(half, PIECES)),
+        12: lambda: rest(pair_down, range(half)),
+        14: lambda: (advance(over_cores, 13), multiply_last()),
     }
-    count = len(TASKS)
-    for t in range(count + 4):
+    lags = ((X_LAG, finish), (Z_LAG, over_z), (PASS_LAG, pass_on), (CORE_LAG, over_cores))
+    for t in range(count + X_LAG):
         if t in before:
             before[t]()
-        if t < count:
+        if t < count - 2:
             multiply(t)
-        if 0 <= t - 1 < count:
-            over_cores(t - 1)
-        if 0 <= t - 2 < count:
-            over_z(t - 2)
-        if 0 <= t - 4 < count:
-            finish(t - 4)
+        for lag, stage in lags:
+            if 0 <= t - lag < count:
+                advance(stage, t - lag)
 
     for copies in (own_up, own_down, own_pair, pair_up, pair_down, on_own, on_pair):
         for copy in copies:
             copy.wait_send()
-    for offset in OFFSETS[1:]:
+    for offset in OFFSETS[8:]:
         a_copy(offset).wait_send()
     for t in (count - 2, count - 1):
         c_copy(t).wait_send()
     for t in range(count):
-        for ez in (1, 2, 3):
-            z_copy(t, ez).wait_send()
+        for k in range(4):
+            z_copy(t, k).wait_send()
         if TASKS[t][1] == 1:
             x_copy(t).wait_send()
 
@@ -244,17 +337,17 @@
     mu_dev, p_dev, nu_all = tensor.shape
     depth, width = coefficients.shape
     count = nu_all // depth
-    amask = jnp.repeat(occupancy.astype(jnp.float32).reshape(count, depth // BLOCK), BLOCK, axis=1)
-    bmask = jnp.repeat(coeff_occupancy.astype(jnp.float32), BLOCK, axis=1)
     panels, tasks = len(PANELS), len(TASKS)
     f32, bf16, dma = jnp.float32, jnp.bfloat16, pltpu.SemaphoreType.DMA
     vmem, hbm = pl.BlockSpec(memory_space=pltpu.VMEM), pl.BlockSpec(memory_space=pl.ANY)
+    smem = pl.BlockSpec(memory_space=pltpu.SMEM)
     result = pl.pallas_call(
         kernel,
         out_shape=jax.ShapeDtypeStruct((mu_dev, panels * width), f32),
-        in_specs=[hbm, vmem, hbm, vmem],
+        in_specs=[hbm, smem, hbm, smem],
         out_specs=vmem,
         scratch_shapes=[
+            pltpu.VMEM((SLOTS, mu_dev, 2 * depth // 128, 128), f32),
             pltpu.VMEM((count, mu_dev, depth), f32),
             pltpu.VMEM((count, mu_dev, depth), f32),
             pltpu.VMEM((count * mu_dev, depth), bf16),
@@ -269,7 +362,7 @@
             pltpu.VMEM((panels, mu_dev, width), f32),
             dma((count,)), dma((count,)), dma((count,)),
             dma((PIECES,)), dma((7, PIECES)), dma((panels, PIECES)),
-            dma((tasks,)), dma((tasks,)), dma((tasks, 3)), dma((tasks, 3)),
+            dma((tasks,)), dma((tasks,)), dma((tasks, 4)), dma((tasks, 4)),
             dma((panels,)), dma((panels,)),
         ],
         compiler_params=pltpu.CompilerParams(
@@ -277,7 +370,7 @@
         cost_estimate=pl.CostEstimate(
             flops=6 * count * mu_dev * depth * panels * width, bytes_accessed=16 * 1024 * 1024, transcendentals=0),
         name="transform",
-    )(tensor.reshape(mu_dev * p_dev, nu_all), amask, coefficients, bmask)
+    )(tensor.reshape(mu_dev, nu_all // 128, 128), occupancy.reshape(1, nu_all // BLOCK), coefficients, coeff_occupancy.T)
     return result.reshape(mu_dev, p_dev, panels * width)
 
 

time: 218 us -> 200 us (0.917)
  local copies, waits for them, and re-layouts: 13.6 us -> 2.82 us
  Pallas kernels: 202 us -> 197 us
    unnamed x1 -> x0, local copies, waits for them, and re-layouts: 9 us -> none
    pallas_call x1, Pallas kernels: 202 us -> 197 us  [on_device(): pl.pallas_call(kernel, out_shape=jax.ShapeDtypeStruct((mu_dev, panels * w...]
where the time goes in v2:
time: 200 us
  Pallas kernels  197 us (98%)
  local copies, waits for them, and re-layouts  2.82 us (1%)
    pallas_call x1, Pallas kernels, on_device(): pl.pallas_call(kernel, out_shape=jax.ShapeDtypeStruct((mu_dev, panels * w...  197 us

profile of v2, /device:TPU:0, one launch (start us, length us, event | category | flops | bytes accessed | tf_op | source)
XLA Modules:
  0.0 199.9 jit_solution(11318362874763143090)
XLA Ops:
  0.0 197.1 %transform.1 = f32[64,3072]{1,0:T(8,128)} custom-call(f32[64,192,128]{2,1,0:T(8,128)} %bitcast.5, s32[1,384]{1,0:T(1,128)} %bitcast.7, f32[1536,384]{1,0:T(8,128)} %b_hbm.1, s32[6,24]{1,0:T(8,128)} %bitcast.6), custom_call_target="tpu_custom_call" | custom-call | flops 28991029248 | bytes 16777216 | tf_op jit(solution)/shard_map/transform/pallas_call | solution.py:344
  197.1 2.8 %copy.5 = f32[64,1,3072]{2,1,0:T(1,128)} copy(f32[64,1,3072]{2,0,1:T(8,128)} %bitcast.4) | data formatting | bytes 1572864 | tf_op jit(solution)/shard_map/reshape | solution.py:374

commit v3 on v2

--- a/solution.py
+++ b/solution.py
@@ -17,7 +17,7 @@
 X_LAG = 7
 OFFSETS = [(ez, eh, ec) for eh in range(2) for ec in range(2) for ez in range(4)]
 PANELS = [(0, 0), (0, 1), (3, 0), (1, 0), (3, 1), (1, 1), (2, 0), (2, 1)]
-TASKS = [(0, 0), (2, 0), (3, 0), (1, 0), (6, 0), (0, 1), (2, 1), (3, 1), (1, 1), (6, 1),
+TASKS = [(0, 0), (2, 0), (3, 0), (1, 0), (6, 0), (6, 1), (0, 1), (2, 1), (3, 1), (1, 1),
          (4, 0), (4, 1), (5, 0), (5, 1), (7, 1), (7, 0)]
 
 
@@ -170,18 +170,19 @@
             blo[rows, :] = (values - high.astype(jnp.float32)).astype(jnp.bfloat16)
             return _
 
-        lax.fori_loop(0, depth // BLOCK, convert, 0)
+        if t == 0 or TASKS[t - 1][0] != n:
+            lax.fori_loop(0, depth // BLOCK, convert, 0)
 
         def tile(m, _):
-            rows = pl.ds(pl.multiple_of(h * 512 + m * 256, 256), 256)
+            rows = pl.ds(pl.multiple_of(h * 512 + m * 512, 512), 512)
             high, low = ahi[rows, :], alo[rows, :]
             total = jnp.dot(low, bhi[...], preferred_element_type=jnp.float32)
             total += jnp.dot(high, blo[...], preferred_element_type=jnp.float32)
             total += jnp.dot(high, bhi[...], preferred_element_type=jnp.float32)
-            cpart[slot, pl.ds(m * 4, 4)] = total.reshape(4, BLOCK, width)
+            cpart[slot, pl.ds(m * 8, 8)] = total.reshape(8, BLOCK, width)
             return _
 
-        lax.fori_loop(0, 2, tile, 0)
+        tile(0, 0)
         c_copy(t).start()
 
     other = (row_of((0, 0, 1)), c)
@@ -304,7 +305,8 @@
         1: lambda: (forward_own(), forward_pair(), rest(own_up, range(half, PIECES)), rest(own_down, range(half))),
         4: lambda: (flush(4), rest(on_own, range(PIECES))),
         5: lambda: (flush(5), take(1)),
-        8: lambda: pass_on_pair((0, 2, 1, 3)),
+        6: lambda: pass_on_pair((0, 2)),
+        7: lambda: pass_on_pair((1, 3)),
         10: lambda: rest(pair_up, range(half, PIECES)),
         12: lambda: rest(pair_down, range(half)),
         14: lambda: (advance(over_cores, 13), multiply_last()),

time: 200 us -> 194 us (0.970)
  Pallas kernels: 197 us -> 191 us
    pallas_call x1, Pallas kernels: 197 us -> 191 us  [on_device(): pl.pallas_call(kernel, out_shape=jax.ShapeDtypeStruct((mu_dev, panels * w...]
where the time goes in v3:
time: 194 us; the launch traced here: 193 us
  Pallas kernels  191 us (98%)
  local copies, waits for them, and re-layouts  2.82 us (1%)
    pallas_call x1, Pallas kernels, on_device(): pl.pallas_call(kernel, out_shape=jax.ShapeDtypeStruct((mu_dev, panels * w...  191 us

profile of v3, /device:TPU:0, one launch (start us, length us, event | category | flops | bytes accessed | tf_op | source)
XLA Modules:
  0.0 193.4 jit_solution(11754483527763771590)
XLA Ops:
  0.0 190.6 %transform.1 = f32[64,3072]{1,0:T(8,128)} custom-call(f32[64,192,128]{2,1,0:T(8,128)} %bitcast.5, s32[1,384]{1,0:T(1,128)} %bitcast.7, f32[1536,384]{1,0:T(8,128)} %b_hbm.1, s32[6,24]{1,0:T(8,128)} %bitcast.6), custom_call_target="tpu_custom_call" | custom-call | flops 28991029248 | bytes 16777216 | tf_op jit(solution)/shard_map/transform/pallas_call | solution.py:346
  190.6 2.8 %copy.5 = f32[64,1,3072]{2,1,0:T(1,128)} copy(f32[64,1,3072]{2,0,1:T(8,128)} %bitcast.4) | data formatting | bytes 1572864 | tf_op jit(solution)/shard_map/reshape | solution.py:376

commit v4 on v3

--- a/solution.py
+++ b/solution.py
@@ -233,8 +233,12 @@
         if n not in [task[0] for task in TASKS[:t]]:
             return
         x_copy(t).wait_recv()
-        cols = pl.ds(pl.multiple_of(col_of(*PANELS[n]) * width, 128), width)
-        out_ref[:, cols] = keep[0, n] + xrecv[n]
+        values = keep[0, n] + xrecv[n]
+        lanes, all_lanes = width // 128, len(PANELS) * width // 128
+        for g in range(BLOCK // 8):
+            for l in range(lanes):
+                rows = pl.ds(g * 8 * all_lanes + col_of(*PANELS[n]) * lanes + l, 8, stride=all_lanes)
+                out_ref[rows, :] = values[g * 8:(g + 1) * 8, l * 128:(l + 1) * 128]
 
     def multiply_last():
         t0 = len(TASKS) - 2
@@ -345,7 +349,7 @@
     smem = pl.BlockSpec(memory_space=pltpu.SMEM)
     result = pl.pallas_call(
         kernel,
-        out_shape=jax.ShapeDtypeStruct((mu_dev, panels * width), f32),
+        out_shape=jax.ShapeDtypeStruct((mu_dev * panels * width // 128, 128), f32),
         in_specs=[hbm, smem, hbm, smem],
         out_specs=vmem,
         scratch_shapes=[

time: 194 us -> 193 us (level)
    reshape x1 -> x0, local copies, waits for them, and re-layouts: 2.82 us -> none  [on_device(): return result.reshape(mu_dev, p_dev, panels * width)]
    unnamed x0 -> x1, local copies, waits for them, and re-layouts: none -> 2.06 us
where the time goes in v4:
time: 193 us
  Pallas kernels  191 us (99%)
  local copies, waits for them, and re-layouts  2.06 us (1%)
    pallas_call x1, Pallas kernels, on_device(): pl.pallas_call(kernel, out_shape=jax.ShapeDtypeStruct((mu_dev * panels *...  191 us

profile of v4, /device:TPU:0, one launch (start us, length us, event | category | flops | bytes accessed | tf_op | source)
XLA Modules:
  0.0 192.7 jit_solution(5557901886180187540)
XLA Ops:
  0.0 190.6 %transform.1 = f32[1536,128]{1,0:T(8,128)} custom-call(f32[64,192,128]{2,1,0:T(8,128)} %bitcast.5, s32[1,384]{1,0:T(1,128)} %bitcast.7, f32[1536,384]{1,0:T(8,128)} %b_hbm.1, s32[6,24]{1,0:T(8,128)} %bitcast.6), custom_call_target="tpu_custom_call" | custom-call | flops 28991029248 | bytes 16777216 | tf_op jit(solution)/shard_map/transform/pallas_call | solution.py:350
  190.6 2.1 %copy.7 = f32[64,1,3072]{2,1,0:T(1,128)} copy(f32[64,1,3072]{2,1,0:T(1,128)} %bitcast.4) | data formatting | bytes 1572864
